TPU v7x, 256 devices: a whole 4x4x8 slice. The times are simulated.
256 devices in a mesh: dp: 4 (over x_lo, core), ctx: 64 (over x_hi, z, y).
Axes of the slice: x: 4 (x_hi: 2, x_lo: 2; x = x_hi * 2 + x_lo), y: 4, z: 8, core: 2. Of those that a mesh axis runs over, the one named last changes fastest.
Arguments:
- queries: bfloat16 [65536, 512], P(('dp', 'ctx')), parts along dimension 0, may hold values from -9 to 9
- keys: bfloat16 [65536, 128], P(('dp', 'ctx')), parts along dimension 0, may hold values from -9 to 9
- values: bfloat16 [65536, 128], P(('dp', 'ctx')), parts along dimension 0, may hold values from -6 to 6
- lengths: int32 [32], P('dp'), parts along dimension 0, may hold values from 1 to 10240, 16384 in all
Outputs:
- attended: bfloat16 [65536, 512], P(('dp', 'ctx')), parts along dimension 0
- log_norm: float32 [4, 65536], P(None, ('dp', 'ctx')), parts along dimension 1
There are 4 independent parts, one for each index of `dp`. A program takes and returns all parts, laid end to end along the dimension named above; each array names one. Nothing has to cross between parts.
Inputs may be any that keep to these rules, and one draw needn't show every extreme that they name: The 8 lengths sum to 16384, and the largest is exactly 10240.
All inputs are finite; a program needn't handle non-finite values.
Results may differ from a plain program's by a relative error of at most 0.0045.
Values may be sent and summed in bfloat16 or wider, within the bound.
No kernel may reach another device: no remote copies, remote signals or barrier semaphores. Data moves between devices by JAX's collectives and lax.ppermute only.
A program may use at most 64 MiB of HBM per device.

v0:
```python
import functools
import math

import jax
import jax.numpy as jnp
from jax import lax
from jax.experimental import pallas as pl
from jax.experimental.pallas import tpu as pltpu
from jax.sharding import PartitionSpec as P

X, Z, Y = 2, 8, 4
ROWS = 256
HEADS = 4
DIM = 128
EXT = DIM + 16
ROW_SPAN = Y * ROWS
BAND = 10
FAR_ROW = 1 << 14
NEG = -1e30
FLOOR = -1e29
CHUNK = 4
EXP2_SCALE = math.log2(math.e) / math.sqrt(DIM)
LOG_2 = math.log(2.0)


def index_of(x, z, y):
    return x * (Z * Y) + (z % Z) * Y + (y % Y)


def y_pairs(step):
    return [
        (index_of(x, z, y), index_of(x, z, y + step))
        for x in range(X)
        for z in range(Z)
        for y in range(Y)
    ]


COLUMNS = range(X)
NEXT = [((c, z), (c, z + 1)) for c in COLUMNS for z in range(Z - 1)]
LOW_NEXT = [((0, z), (1, (z + 1) % Z)) for z in range(Z)]
BACK = [((0, z), (1, z - 1)) for z in range(1, Z)] + [((c, 0), (c, Z - 1)) for c in COLUMNS]
HALF = [((c, z), (c, z + 4)) for c in COLUMNS for z in range(4)]
HALF += [((0, z), (1, z - 4)) for z in range(4, Z)]
EXTRA_ONE = [((c, 1), (c, Z - 1)) for c in COLUMNS]
EXTRA_FOUR = [((c, 4), (c, Z - 1)) for c in COLUMNS] + [((0, 3), (1, 0))]
UP = [((0, z), (0, z + 1)) for z in range(1, Z - 1)] + [((1, z), (1, (z + 1) % Z)) for z in range(Z)]
DOWN = [((0, z), (0, z - 1)) for z in range(4, Z)] + [((1, z), (1, (z - 1) % Z)) for z in range(Z)]


def move(block, pairs):
    along = [(index_of(*a, y), index_of(*b, y)) for a, b in pairs for y in range(Y)]
    return lax.ppermute(block, "ctx", along)


def own_row(step):
    return lambda x, z: x * Z + (z + step + Z) % Z


def low_row(step):
    return lambda x, z: jnp.where(x == 1, (z + step + Z) % Z, FAR_ROW)


def half_row(step):
    def row(x, z):
        at = x * Z + (z + step + Z) % Z - 4
        return jnp.where(at >= 0, at, FAR_ROW)

    return row


def back_row(step):
    def row(x, z):
        via = (z + step + Z) % Z
        return jnp.where(x == 1, via + 1, jnp.where(via == Z - 1, 0, FAR_ROW))

    return row


def extra_one_row(x, z):
    return jnp.where(z == Z - 1, x * Z + 1, FAR_ROW)


def extra_four_row(x, z):
    return jnp.where(z == Z - 1, x * Z + 4, jnp.where((z == 0) & (x == 1), 3, FAR_ROW))


def gather(block):
    below, low_next = move(block, NEXT), move(block, LOW_NEXT)
    back, half = move(block, BACK), move(block, HALF)
    extra_one, extra_four = move(block, EXTRA_ONE), move(block, EXTRA_FOUR)
    up = move(jnp.concatenate([below, low_next, half], 0), UP)
    down = move(jnp.concatenate([back, half, low_next], 0), DOWN)
    first = [
        (block, [own_row(0)]),
        (below, [own_row(-1)]),
        (low_next, [low_row(-1)]),
        (back, [back_row(0)]),
        (half, [half_row(0)]),
        (extra_one, [extra_one_row]),
        (extra_four, [extra_four_row]),
    ]
    second = [(up, [own_row(-2), low_row(-2), half_row(-1)]), (down, [back_row(1), half_row(1), low_row(0)])]
    return first, second


def doc_start(lengths_ref, position):
    start = position * 0
    end = jnp.int32(0)
    for k in range(8):
        size = lengths_ref[k]
        end = end + size
        start = start + jnp.where(position >= end, size, 0)
    return start


def attend(steps, places, carried, finish, tile, *refs):
    nq = len(steps)
    flat = [p for group in places for p in group]
    nb = len(flat)
    refs = list(refs)
    lengths_ref = refs.pop(0)
    q_refs = [refs.pop(0) for _ in range(nq)]
    kv_refs = [refs.pop(0) for _ in places]
    if carried:
        acc_in, top_in = refs.pop(0), refs.pop(0)
    if finish:
        message_refs = [refs.pop(0) for _ in range(nq)]
        acc, top = refs.pop(), refs.pop()
    else:
        acc, top = refs.pop(0), refs.pop(0)
    qt, ks, vt, key_at, seen = refs

    me = lax.axis_index("ctx")
    x, z, y = me // (Z * Y), (me // Y) % Z, me % Y
    row = x * Z + z
    row_low = row * ROW_SPAN
    row_high = row_low + (ROW_SPAN - 1)
    low = doc_start(lengths_ref, row_low)

    for n in range(nq):
        for h in range(HEADS):
            scaled = q_refs[n][:, h * DIM : (h + 1) * DIM].T.astype(jnp.float32) * EXP2_SCALE
            high = scaled.astype(jnp.bfloat16)
            qt[n * HEADS + h, :DIM] = high
            qt[n * HEADS + h, DIM:] = (scaled - high.astype(jnp.float32)).astype(jnp.bfloat16)

    for d in range(BAND + 2):
        seen[d] = 0
    for n in range(nb):
        key_at[n] = -FAR_ROW * ROW_SPAN
    starts, places_of = [], []
    for row_of in flat:
        row_from = row_of(x, z)
        k0 = row_from * ROW_SPAN + y * ROWS
        counts = (k0 <= row_high) & (k0 + (ROWS - 1) >= low)
        place = jnp.where(counts, row - row_from, BAND + 1)
        seen[place] = 1
        starts.append(k0)
        places_of.append(place)
    n_slots = jnp.int32(0)
    for d in range(BAND + 1):
        here = seen[d]
        seen[d] = n_slots
        n_slots = n_slots + here
    n = 0
    for ref, group in zip(kv_refs, places):
        for part in range(len(group)):

            @pl.when(places_of[n] <= BAND)
            def _(ref=ref, part=part, k0=starts[n], place=places_of[n]):
                slot = seen[place]
                base = 2 * part * ROWS
                key_at[slot] = k0
                at = pl.multiple_of(slot * ROWS, ROWS)
                for half in range(2):
                    ks[pl.ds(at, ROWS), half * DIM : (half + 1) * DIM] = ref[base : base + ROWS, :]
                for half in range(2):
                    rows = base + ROWS + half * DIM
                    vt[:DIM, pl.ds(pl.multiple_of(at + half * DIM, DIM), DIM)] = ref[rows : rows + DIM, :]

            n += 1
    vt[DIM:, :] = jnp.ones((EXT - DIM, nb * ROWS), jnp.bfloat16)

    if carried:
        acc[...] = acc_in[tile : tile + nq * HEADS]
        top[...] = top_in[tile : tile + nq * HEADS]
    else:
        acc[...] = jnp.zeros(acc.shape, jnp.float32)
        top[...] = jnp.full(top.shape, FLOOR, jnp.float32)

    def one_query_block(qb, _):
        t0 = qb * HEADS
        step = steps[0]
        for n in range(1, nq):
            step = jnp.where(qb == n, steps[n], step)
        q0 = row_low + ((y + step + Y) % Y) * ROWS
        first = doc_start(lengths_ref, q0)
        last = doc_start(lengths_ref, q0 + (ROWS - 1))

        def update(slot, count, masked):
            at = pl.ds(pl.multiple_of(slot * ROWS, ROWS), count * ROWS)
            k, v = ks[at, :], vt[:, at]
            if masked:
                query_pos = q0 + lax.broadcasted_iota(jnp.int32, (1, ROWS), 1)
                query_start = doc_start(lengths_ref, query_pos)
                key_pos = [
                    key_at[slot + i] + lax.broadcasted_iota(jnp.int32, (ROWS, ROWS), 0)
                    for i in range(count)
                ]
                key_pos = jnp.concatenate(key_pos, 0)
                allowed = (key_pos >= query_start) & (key_pos <= query_pos)
            olds = [top[t0 + h] for h in range(HEADS)]
            scores = [
                jnp.dot(k, qt[t0 + h], preferred_element_type=jnp.float32) for h in range(HEADS)
            ]
            if masked:
                scores = [jnp.where(allowed, s, NEG) for s in scores]
            news = [
                jnp.maximum(o, jnp.max(s, axis=0, keepdims=True)) for o, s in zip(olds, scores)
            ]
            weights = [
                jnp.exp2(s - n).astype(jnp.bfloat16) for s, n in zip(scores, news)
            ]
            sums = [jnp.dot(v, w, preferred_element_type=jnp.float32) for w in weights]
            sums = [
                acc[t0 + h] * jnp.exp2(olds[h] - news[h]) + sums[h]
                for h in range(HEADS)
            ]
            for h in range(HEADS):
                top[t0 + h] = news[h]
                acc[t0 + h] = sums[h]

        begin, near, inside, reach = (jnp.int32(0) for _ in range(4))
        for n in range(nb):
            k0 = key_at[n]
            begin = begin + jnp.where(k0 > q0 + (ROWS - 1), 1, 0)
            near = near + jnp.where(k0 + (ROWS - 1) > q0, 1, 0)
            inside = inside + jnp.where(k0 >= last, 1, 0)
            reach = reach + jnp.where(k0 + (ROWS - 1) >= first, 1, 0)

        def chunk(at, size):
            whole = (at >= near) & (at + size <= inside)
            pl.when(whole)(functools.partial(update, at, size, False))
            pl.when(jnp.logical_not(whole))(functools.partial(update, at, size, True))

        times = jnp.maximum(reach - begin, 0) // CHUNK

        def one_chunk(c, _):
            chunk(begin + c * CHUNK, CHUNK)
            return 0

        lax.fori_loop(0, times, one_chunk, 0)
        at = begin + times * CHUNK
        size = CHUNK // 2
        while size:
            some = reach - at >= size
            pl.when(some)(functools.partial(chunk, at, size))
            at = at + jnp.where(some, size, 0)
            size //= 2
        return 0

    lax.fori_loop(0, nq, one_query_block, 0)

    if finish:
        for n in range(nq):
            for h in range(HEADS):
                t = n * HEADS + h
                at = slice(h * ROWS, (h + 1) * ROWS)
                total = acc[t, DIM : DIM + 1]
                some = total > 0
                total = jnp.where(some, total, 1.0)
                log_norm = jnp.where(some, top[t] * LOG_2 + jnp.log(total), NEG)
                message_refs[n][:DIM, at] = (acc[t, :DIM] * (1.0 / total)).astype(jnp.bfloat16)
                first = log_norm.astype(jnp.bfloat16)
                rest = log_norm - first.astype(jnp.float32)
                second = rest.astype(jnp.bfloat16)
                third = (rest - second.astype(jnp.float32)).astype(jnp.bfloat16)
                row = lax.broadcasted_iota(jnp.int32, (EXT - DIM, ROWS), 0)
                pieces = jnp.where(
                    row == 0,
                    first.astype(jnp.float32),
                    jnp.where(row == 1, second.astype(jnp.float32), third.astype(jnp.float32)),
                )
                message_refs[n][DIM:, at] = pieces.astype(jnp.bfloat16)


def run_attend(lengths, queries, steps, arrays, places, carry, finish, tile=0):
    nq, nb = len(steps), sum(len(g) for g in places)
    tiles = nq * HEADS
    vmem = pl.BlockSpec(memory_space=pltpu.VMEM)
    acc = jax.ShapeDtypeStruct((tiles, EXT, ROWS), jnp.float32)
    top = jax.ShapeDtypeStruct((tiles, 1, ROWS), jnp.float32)
    scratch = [
        pltpu.VMEM((tiles, 2 * DIM, ROWS), jnp.bfloat16),
        pltpu.VMEM((nb * ROWS, 2 * DIM), jnp.bfloat16),
        pltpu.VMEM((EXT, nb * ROWS), jnp.bfloat16),
        pltpu.SMEM((nb,), jnp.int32),
        pltpu.SMEM((BAND + 2,), jnp.int32),
    ]
    if finish:
        out_shape = [jax.ShapeDtypeStruct((EXT, HEADS * ROWS), jnp.bfloat16)] * nq
        scratch += [pltpu.VMEM(top.shape, top.dtype), pltpu.VMEM(acc.shape, acc.dtype)]
    else:
        out_shape = [acc, top]
    operands = [lengths, *queries, *arrays, *(carry or ())]
    units = 5 * nq * nb * HEADS * ROWS * ROWS
    return pl.pallas_call(
        functools.partial(attend, steps, places, carry is not None, finish, tile),
        out_shape=out_shape,
        in_specs=[pl.BlockSpec(memory_space=pltpu.SMEM)] + [vmem] * (len(operands) - 1),
        out_specs=[vmem] * len(out_shape),
        scratch_shapes=scratch,
        compiler_params=pltpu.CompilerParams(vmem_limit_bytes=28 << 20),
        cost_estimate=pl.CostEstimate(
            flops=units * DIM * 2, bytes_accessed=1 << 20, transcendentals=units // 2
        ),
    )(*operands)


def turn_values(k_ref, v_ref, out_ref):
    out_ref[:ROWS, :] = k_ref[...]
    for half in range(2):
        at = ROWS + half * DIM
        out_ref[at : at + DIM, :] = v_ref[half * DIM : (half + 1) * DIM, :].T


def run_turn(kernel, shape, *operands):
    vmem = pl.BlockSpec(memory_space=pltpu.VMEM)
    return pl.pallas_call(
        kernel,
        out_shape=jax.ShapeDtypeStruct(shape, jnp.bfloat16),
        in_specs=[vmem] * len(operands),
        out_specs=vmem,
    )(*operands)


def merge(acc, top, *refs):
    *received, out, norm = refs
    for h in range(HEADS):
        at = slice(h * ROWS, (h + 1) * ROWS)
        own_total = acc[h, DIM : DIM + 1]
        logs = [top[h] * LOG_2 + jnp.log(own_total)]
        for r in received:
            pieces = r[DIM:, at].astype(jnp.float32)
            logs.append(pieces[0:1] + pieces[1:2] + pieces[2:3])
        most = functools.reduce(jnp.maximum, logs)
        parts = [jnp.exp(v - most) for v in logs]
        total = sum(parts)
        mixed = acc[h, :DIM] * (parts[0] / (own_total * total))
        for r, part in zip(received, parts[1:]):
            mixed = mixed + r[:DIM, at].astype(jnp.float32) * (part / total)
        out[:, h * DIM : (h + 1) * DIM] = mixed.T.astype(jnp.bfloat16)
        norm[h : h + 1, :] = most + jnp.log(total)


def run_merge(acc, top, received):
    vmem = pl.BlockSpec(memory_space=pltpu.VMEM)
    return pl.pallas_call(
        merge,
        out_shape=[
            jax.ShapeDtypeStruct((ROWS, HEADS * DIM), jnp.bfloat16),
            jax.ShapeDtypeStruct((HEADS, ROWS), jnp.float32),
        ],
        in_specs=[vmem] * (2 + len(received)),
        out_specs=[vmem] * 2,
        compiler_params=pltpu.CompilerParams(vmem_limit_bytes=24 << 20),
    )(acc, top, *received)


def shards(queries, keys, values, lengths):
    block = run_turn(turn_values, (2 * ROWS, DIM), keys, values)
    most, rest = gather(block)
    unzip = lambda pairs: ([a for a, _ in pairs], [p for _, p in pairs])
    steps = (-1, 1, 2)
    others = [lax.ppermute(queries, "ctx", y_pairs(-s)) for s in steps]
    received = []
    for low, high in ((0, 2), (2, 3)):
        group, these = steps[low:high], others[low:high]
        carry = run_attend(lengths, these, group, *unzip(most), None, False)
        messages = run_attend(lengths, these, group, *unzip(rest), carry, True)
        received += [lax.ppermute(m, "ctx", y_pairs(s)) for m, s in zip(messages, group)]
    acc, top = run_attend(lengths, [queries], (0,), *unzip(most + rest), None, False)
    return tuple(run_merge(acc, top, received))


def solution(mesh):
    in_specs = (P(("dp", "ctx"), None), P(("dp", "ctx"), None), P(("dp", "ctx"), None), P("dp"))
    out_specs = (P(("dp", "ctx"), None), P(None, ("dp", "ctx")))
    return jax.shard_map(shards, mesh=mesh, in_specs=in_specs, out_specs=out_specs, check_vma=False)
```

profile of v0, /device:TPU:6, one launch (start us, length us, event | category | flops | bytes accessed | tf_op | source)
XLA Modules:
  0.0 64.9 jit_solution(13374220476380693388)
XLA Ops:
  0.6 1.6 %shard_map.59.refs_2_.refs_3_ = bf16[512,128]{1,0:T(8,128)(2,1)} custom-call(bf16[256,128]{1,0:T(8,128)(2,1)} %k_ref.1, bf16[256,128]{1,0:T(8,128)(2,1)} %v_ref.1), custom_call_target="tpu_custom_call" | custom-call | tf_op jit(solution)/shard_map/pallas_call | solution.py:330
  2.2 3.9 %collective-permute-start = (bf16[512,128]{1,0:T(8,128)(2,1)}, bf16[512,128]{1,0:T(8,128)(2,1)S(1)}, u32[]{:S(2)}, u32[]{:S(2)}) collective-permute-start(bf16[512,128]{1,0:T(8,128)(2,1)} %shard_map.59.refs_2_.refs_3_), channel_id=1, source_target_pairs={{0,4},{1,5},{2,6},{3,7},{4,8},{5,9},{6,10},{7,11},{8,12},{9,13},{1... | collective-permute-start | bytes 393224 | tf_op jit(solution)/shard_map/ppermute | solution.py:53
  6.2 1.3 %collective-permute-start.1 = (bf16[512,128]{1,0:T(8,128)(2,1)}, bf16[512,128]{1,0:T(8,128)(2,1)S(1)}, u32[]{:S(2)}, u32[]{:S(2)}) collective-permute-start(bf16[512,128]{1,0:T(8,128)(2,1)} %shard_map.59.refs_2_.refs_3_), channel_id=1, source_target_pairs={{0,36},{1,37},{2,38},{3,39},{4,40},{5,41},{6,42},{7,43},{8,44},{9,... | collective-permute-start | bytes 393224 | tf_op jit(solution)/shard_map/ppermute | solution.py:53
  7.5 5.2 %collective-permute-start.2 = (bf16[512,128]{1,0:T(8,128)(2,1)}, bf16[512,128]{1,0:T(8,128)(2,1)S(1)}, u32[]{:S(2)}, u32[]{:S(2)}) collective-permute-start(bf16[512,128]{1,0:T(8,128)(2,1)} %shard_map.59.refs_2_.refs_3_), channel_id=1, source_target_pairs={{4,32},{5,33},{6,34},{7,35},{8,36},{9,37},{10,38},{11,39},{12,40},... | collective-permute-start | bytes 393224 | tf_op jit(solution)/shard_map/ppermute | solution.py:53
  12.7 4.3 %collective-permute-start.3 = (bf16[512,128]{1,0:T(8,128)(2,1)}, bf16[512,128]{1,0:T(8,128)(2,1)S(1)}, u32[]{:S(2)}, u32[]{:S(2)}) collective-permute-start(bf16[512,128]{1,0:T(8,128)(2,1)} %shard_map.59.refs_2_.refs_3_), channel_id=1, source_target_pairs={{0,16},{1,17},{2,18},{3,19},{4,20},{5,21},{6,22},{7,23},{8,24},{9,... | collective-permute-start | bytes 393224 | tf_op jit(solution)/shard_map/ppermute | solution.py:53
  17.0 3.3 %collective-permute-start.12 = (bf16[256,512]{1,0:T(8,128)(2,1)}, bf16[256,512]{1,0:T(8,128)(2,1)S(1)}, u32[]{:S(2)}, u32[]{:S(2)}) collective-permute-start(bf16[256,512]{1,0:T(8,128)(2,1)} %refs_1_.1), channel_id=1, source_target_pairs={{0,2},{1,3},{2,0},{3,1},{4,6},{5,7},{6,4},{7,5},{8,10},{9,11},{10,... | collective-permute-start | bytes 786440 | tf_op jit(solution)/shard_map/ppermute | solution.py:376
  20.3 0.7 %collective-permute-start.4 = (bf16[512,128]{1,0:T(8,128)(2,1)}, bf16[512,128]{1,0:T(8,128)(2,1)S(1)}, u32[]{:S(2)}, u32[]{:S(2)}) collective-permute-start(bf16[512,128]{1,0:T(8,128)(2,1)} %shard_map.59.refs_2_.refs_3_), channel_id=1, source_target_pairs={{4,28},{5,29},{6,30},{7,31},{36,60},{37,61},{38,62},{39,63},{68,92... | collective-permute-start | bytes 393224 | tf_op jit(solution)/shard_map/ppermute | solution.py:53
  21.0 1.3 %collective-permute-start.5 = (bf16[512,128]{1,0:T(8,128)(2,1)}, bf16[512,128]{1,0:T(8,128)(2,1)S(1)}, u32[]{:S(2)}, u32[]{:S(2)}) collective-permute-start(bf16[512,128]{1,0:T(8,128)(2,1)} %shard_map.59.refs_2_.refs_3_), channel_id=1, source_target_pairs={{16,28},{17,29},{18,30},{19,31},{48,60},{49,61},{50,62},{51,63},{1... | collective-permute-start | bytes 393224 | tf_op jit(solution)/shard_map/ppermute | solution.py:53
  22.3 0.8 %collective-permute-start.8 = (bf16[256,512]{1,0:T(8,128)(2,1)}, bf16[256,512]{1,0:T(8,128)(2,1)S(1)}, u32[]{:S(2)}, u32[]{:S(2)}) collective-permute-start(bf16[256,512]{1,0:T(8,128)(2,1)} %refs_1_.1), channel_id=1, source_target_pairs={{0,1},{1,2},{2,3},{3,0},{4,5},{5,6},{6,7},{7,4},{8,9},{9,10},{10,1... | collective-permute-start | bytes 786440 | tf_op jit(solution)/shard_map/ppermute | solution.py:376
  23.0 5.4 %collective-permute-done.3.refs_6_.refs_7_ = bf16[512,128]{1,0:T(8,128)(2,1)S(1)} collective-permute-done((bf16[512,128]{1,0:T(8,128)(2,1)}, bf16[512,128]{1,0:T(8,128)(2,1)S(1)}, u32[]{:S(2)}, u32[]{:S(2)}) %collective-permute-start.3) | collective-permute-done | bytes 131104 | tf_op jit(solution)/shard_map/ppermute | solution.py:53
  28.5 3.2 %collective-permute-start.9 = (bf16[256,512]{1,0:T(8,128)(2,1)}, bf16[256,512]{1,0:T(8,128)(2,1)S(1)}, u32[]{:S(2)}, u32[]{:S(2)}) collective-permute-start(bf16[256,512]{1,0:T(8,128)(2,1)} %refs_1_.1), channel_id=1, source_target_pairs={{0,3},{1,0},{2,1},{3,2},{4,7},{5,4},{6,5},{7,6},{8,11},{9,8},{10,9... | collective-permute-start | bytes 786440 | tf_op jit(solution)/shard_map/ppermute | solution.py:376
  31.7 3.3 %collective-permute-start.6 = (bf16[1536,128]{1,0:T(8,128)(2,1)S(1)}, bf16[1536,128]{1,0:T(8,128)(2,1)S(1)}, u32[]{:S(2)}, u32[]{:S(2)}) collective-permute-start(bf16[1536,128]{1,0:T(8,128)(2,1)S(1)} %get-tuple-element.19), channel_id=1, source_target_pairs={{4,8},{5,9},{6,10},{7,11},{8,12},{9,13},{10,14},{11,15},{12,16},{1... | collective-permute-start | bytes 1179656 | tf_op jit(solution)/shard_map/ppermute | solution.py:53
  35.0 3.8 %collective-permute-start.7 = (bf16[1536,128]{1,0:T(8,128)(2,1)S(1)}, bf16[1536,128]{1,0:T(8,128)(2,1)S(1)}, u32[]{:S(2)}, u32[]{:S(2)}) collective-permute-start(bf16[1536,128]{1,0:T(8,128)(2,1)S(1)} %get-tuple-element.18), channel_id=1, source_target_pairs={{16,12},{17,13},{18,14},{19,15},{20,16},{21,17},{22,18},{23,19},{2... | collective-permute-start | bytes 1179656 | tf_op jit(solution)/shard_map/ppermute | solution.py:53
  38.8 3.1 %shard_map.63 = (f32[4,144,256]{2,1,0:T(8,128)S(1)}, f32[4,1,256]{2,1,0:T(1,128)S(1)}) custom-call(s32[8]{0:T(128)S(1)} %copy-done.2, bf16[256,512]{1,0:T(8,128)(2,1)S(1)} %collective-permute-done.12.refs_1_, bf16[512,128]{1,0:T(8,128)(2,1)S(1)} %copy-done, bf16[512,128]{1,0:T(8,128)(2,1)S(1)} %collective-permute-done.refs_3_.refs_4_, ...), custom_call_target="tpu_custom_call" | custom-call | flops 2348810240 | bytes 1048576 | tf_op jit(solution)/shard_map/pallas_call | solution.py:308
  41.9 5.6 %shard_map.61 = (f32[8,144,256]{2,1,0:T(8,128)S(1)}, f32[8,1,256]{2,1,0:T(1,128)S(1)}) custom-call(s32[8]{0:T(128)S(1)} %copy-done.2, bf16[256,512]{1,0:T(8,128)(2,1)S(1)} %collective-permute-done.8.refs_1_, bf16[256,512]{1,0:T(8,128)(2,1)S(1)} %collective-permute-done.9.refs_2_, bf16[512,128]{1,0:T(8,128)(2,1)S(1)} %copy-done, ...), custom_call_target="tpu_custom_call" | custom-call | flops 4697620480 | bytes 1048576 | tf_op jit(solution)/shard_map/pallas_call | solution.py:308
  47.6 2.4 %shard_map.64 = bf16[144,1024]{1,0:T(8,128)(2,1)S(1)} custom-call(s32[8]{0:T(128)S(1)} %copy-done.2, bf16[256,512]{1,0:T(8,128)(2,1)S(1)} %collective-permute-done.12.refs_1_, bf16[1536,128]{1,0:T(8,128)(2,1)S(1)} %collective-permute-done.6.refs_9_.refs_3_.refs_2_, bf16[1536,128]{1,0:T(8,128)(2,1)S(1)} %collective-permute-done.7.refs_10_.refs_4_.refs_3_, ...), custom_call_target="tpu_custom_call" | custom-call | flops 2013265920 | bytes 1048576 | tf_op jit(solution)/shard_map/pallas_call | solution.py:308
  50.0 0.1 collective-permute-start.13
  50.1 4.4 %shard_map.62 = (bf16[144,1024]{1,0:T(8,128)(2,1)S(1)}, bf16[144,1024]{1,0:T(8,128)(2,1)S(1)}) custom-call(s32[8]{0:T(128)S(1)} %copy-done.2, bf16[256,512]{1,0:T(8,128)(2,1)S(1)} %collective-permute-done.8.refs_1_, bf16[256,512]{1,0:T(8,128)(2,1)S(1)} %collective-permute-done.9.refs_2_, ...), custom_call_target="tpu_custom_call" | custom-call | flops 4026531840 | bytes 1048576 | tf_op jit(solution)/shard_map/pallas_call | solution.py:308
  54.5 1.5 %collective-permute-start.10 = (bf16[144,1024]{1,0:T(8,128)(2,1)S(1)}, bf16[144,1024]{1,0:T(8,128)(2,1)S(1)}, u32[]{:S(2)}, u32[]{:S(2)}) collective-permute-start(bf16[144,1024]{1,0:T(8,128)(2,1)S(1)} %get-tuple-element.14), channel_id=1, source_target_pairs={{0,3},{1,0},{2,1},{3,2},{4,7},{5,4},{6,5},{7,6},{8,11},{9,8},{10,9... | collective-permute-start | bytes 884744 | tf_op jit(solution)/shard_map/ppermute | solution.py:382
  56.0 0.6 collective-permute-start.11
  56.6 4.3 %shard_map.60 = (f32[4,144,256]{2,1,0:T(8,128)S(1)}, f32[4,1,256]{2,1,0:T(1,128)S(1)}) custom-call(s32[8]{0:T(128)S(1)} %copy-done.2, bf16[256,512]{1,0:T(8,128)(2,1)S(1)} %copy-done.1, bf16[512,128]{1,0:T(8,128)(2,1)S(1)} %copy-done, bf16[512,128]{1,0:T(8,128)(2,1)S(1)} %collective-permute-done.refs_3_.refs_4_, ...), custom_call_target="tpu_custom_call" | custom-call | flops 4362076160 | bytes 1048576 | tf_op jit(solution)/shard_map/pallas_call | solution.py:308
  60.9 0.5 collective-permute-done.10.refs_0_
  61.4 2.5 %collective-permute-done.11.refs_1_ = bf16[144,1024]{1,0:T(8,128)(2,1)S(1)} collective-permute-done((bf16[144,1024]{1,0:T(8,128)(2,1)S(1)}, bf16[144,1024]{1,0:T(8,128)(2,1)S(1)}, u32[]{:S(2)}, u32[]{:S(2)}) %collective-permute-start.11) | collective-permute-done | bytes 294944 | tf_op jit(solution)/shard_map/ppermute | solution.py:382
  63.9 1.0 %shard_map.65 = (bf16[256,512]{1,0:T(8,128)(2,1)}, f32[4,256]{1,0:T(4,128)}) custom-call(f32[4,144,256]{2,1,0:T(8,128)S(1)} %get-tuple-element.10.acc, f32[4,1,256]{2,1,0:T(1,128)S(1)} %get-tuple-element.11.top, bf16[144,1024]{1,0:T(8,128)(2,1)S(1)} %collective-permute-done.10.refs_0_, bf16[144,1024]{1,0:T(8,128)(2,1)S(1)} %collective-permute-done.11.refs_1_, ...), custom_call_target="tpu_custom_call" | custom-call | tf_op jit(solution)/shard_map/pallas_call | solution.py:359
  (18 shorter events, 0.1 us)
Async XLA Ops:
  0.6 38.2 %copy-start.2 = (s32[8]{0:T(128)S(1)}, s32[8]{0:T(128)}, u32[]{:S(2)}) copy-start(s32[8]{0:T(128)} %refs_0_.9) | copy-start | bytes 100
  2.2 36.6 %copy-start = (bf16[512,128]{1,0:T(8,128)(2,1)S(1)}, bf16[512,128]{1,0:T(8,128)(2,1)}, u32[]{:S(2)}) copy-start(bf16[512,128]{1,0:T(8,128)(2,1)} %shard_map.59.refs_2_.refs_3_) | copy-start | bytes 393220
  2.2 18.0 %collective-permute-start = (bf16[512,128]{1,0:T(8,128)(2,1)}, bf16[512,128]{1,0:T(8,128)(2,1)S(1)}, u32[]{:S(2)}, u32[]{:S(2)}) collective-permute-start(bf16[512,128]{1,0:T(8,128)(2,1)} %shard_map.59.refs_2_.refs_3_), channel_id=1, source_target_pairs={{0,4},{1,5},{2,6},{3,7},{4,8},{5,9},{6,10},{7,11},{8,12},{9,13},{1... | collective-permute-start | bytes 393224 | tf_op jit(solution)/shard_map/ppermute | solution.py:53
  6.2 14.8 %collective-permute-start.1 = (bf16[512,128]{1,0:T(8,128)(2,1)}, bf16[512,128]{1,0:T(8,128)(2,1)S(1)}, u32[]{:S(2)}, u32[]{:S(2)}) collective-permute-start(bf16[512,128]{1,0:T(8,128)(2,1)} %shard_map.59.refs_2_.refs_3_), channel_id=1, source_target_pairs={{0,36},{1,37},{2,38},{3,39},{4,40},{5,41},{6,42},{7,43},{8,44},{9,... | collective-permute-start | bytes 393224 | tf_op jit(solution)/shard_map/ppermute | solution.py:53
  7.5 14.8 %collective-permute-start.2 = (bf16[512,128]{1,0:T(8,128)(2,1)}, bf16[512,128]{1,0:T(8,128)(2,1)S(1)}, u32[]{:S(2)}, u32[]{:S(2)}) collective-permute-start(bf16[512,128]{1,0:T(8,128)(2,1)} %shard_map.59.refs_2_.refs_3_), channel_id=1, source_target_pairs={{4,32},{5,33},{6,34},{7,35},{8,36},{9,37},{10,38},{11,39},{12,40},... | collective-permute-start | bytes 393224 | tf_op jit(solution)/shard_map/ppermute | solution.py:53
  12.7 15.7 %collective-permute-start.3 = (bf16[512,128]{1,0:T(8,128)(2,1)}, bf16[512,128]{1,0:T(8,128)(2,1)S(1)}, u32[]{:S(2)}, u32[]{:S(2)}) collective-permute-start(bf16[512,128]{1,0:T(8,128)(2,1)} %shard_map.59.refs_2_.refs_3_), channel_id=1, source_target_pairs={{0,16},{1,17},{2,18},{3,19},{4,20},{5,21},{6,22},{7,23},{8,24},{9,... | collective-permute-start | bytes 393224 | tf_op jit(solution)/shard_map/ppermute | solution.py:53
  17.0 21.8 %collective-permute-start.12 = (bf16[256,512]{1,0:T(8,128)(2,1)}, bf16[256,512]{1,0:T(8,128)(2,1)S(1)}, u32[]{:S(2)}, u32[]{:S(2)}) collective-permute-start(bf16[256,512]{1,0:T(8,128)(2,1)} %refs_1_.1), channel_id=1, source_target_pairs={{0,2},{1,3},{2,0},{3,1},{4,6},{5,7},{6,4},{7,5},{8,10},{9,11},{10,... | collective-permute-start | bytes 786440 | tf_op jit(solution)/shard_map/ppermute | solution.py:376
  20.3 11.4 %collective-permute-start.4 = (bf16[512,128]{1,0:T(8,128)(2,1)}, bf16[512,128]{1,0:T(8,128)(2,1)S(1)}, u32[]{:S(2)}, u32[]{:S(2)}) collective-permute-start(bf16[512,128]{1,0:T(8,128)(2,1)} %shard_map.59.refs_2_.refs_3_), channel_id=1, source_target_pairs={{4,28},{5,29},{6,30},{7,31},{36,60},{37,61},{38,62},{39,63},{68,92... | collective-permute-start | bytes 393224 | tf_op jit(solution)/shard_map/ppermute | solution.py:53
  21.0 14.1 %collective-permute-start.5 = (bf16[512,128]{1,0:T(8,128)(2,1)}, bf16[512,128]{1,0:T(8,128)(2,1)S(1)}, u32[]{:S(2)}, u32[]{:S(2)}) collective-permute-start(bf16[512,128]{1,0:T(8,128)(2,1)} %shard_map.59.refs_2_.refs_3_), channel_id=1, source_target_pairs={{16,28},{17,29},{18,30},{19,31},{48,60},{49,61},{50,62},{51,63},{1... | collective-permute-start | bytes 393224 | tf_op jit(solution)/shard_map/ppermute | solution.py:53
  22.3 19.7 %collective-permute-start.8 = (bf16[256,512]{1,0:T(8,128)(2,1)}, bf16[256,512]{1,0:T(8,128)(2,1)S(1)}, u32[]{:S(2)}, u32[]{:S(2)}) collective-permute-start(bf16[256,512]{1,0:T(8,128)(2,1)} %refs_1_.1), channel_id=1, source_target_pairs={{0,1},{1,2},{2,3},{3,0},{4,5},{5,6},{6,7},{7,4},{8,9},{9,10},{10,1... | collective-permute-start | bytes 786440 | tf_op jit(solution)/shard_map/ppermute | solution.py:376
  28.5 13.5 %collective-permute-start.9 = (bf16[256,512]{1,0:T(8,128)(2,1)}, bf16[256,512]{1,0:T(8,128)(2,1)S(1)}, u32[]{:S(2)}, u32[]{:S(2)}) collective-permute-start(bf16[256,512]{1,0:T(8,128)(2,1)} %refs_1_.1), channel_id=1, source_target_pairs={{0,3},{1,0},{2,1},{3,2},{4,7},{5,4},{6,5},{7,6},{8,11},{9,8},{10,9... | collective-permute-start | bytes 786440 | tf_op jit(solution)/shard_map/ppermute | solution.py:376
  31.7 15.9 %collective-permute-start.6 = (bf16[1536,128]{1,0:T(8,128)(2,1)S(1)}, bf16[1536,128]{1,0:T(8,128)(2,1)S(1)}, u32[]{:S(2)}, u32[]{:S(2)}) collective-permute-start(bf16[1536,128]{1,0:T(8,128)(2,1)S(1)} %get-tuple-element.19), channel_id=1, source_target_pairs={{4,8},{5,9},{6,10},{7,11},{8,12},{9,13},{10,14},{11,15},{12,16},{1... | collective-permute-start | bytes 1179656 | tf_op jit(solution)/shard_map/ppermute | solution.py:53
  35.0 12.6 %collective-permute-start.7 = (bf16[1536,128]{1,0:T(8,128)(2,1)S(1)}, bf16[1536,128]{1,0:T(8,128)(2,1)S(1)}, u32[]{:S(2)}, u32[]{:S(2)}) collective-permute-start(bf16[1536,128]{1,0:T(8,128)(2,1)S(1)} %get-tuple-element.18), channel_id=1, source_target_pairs={{16,12},{17,13},{18,14},{19,15},{20,16},{21,17},{22,18},{23,19},{2... | collective-permute-start | bytes 1179656 | tf_op jit(solution)/shard_map/ppermute | solution.py:53
  50.0 10.9 %collective-permute-start.13 = (bf16[144,1024]{1,0:T(8,128)(2,1)S(1)}, bf16[144,1024]{1,0:T(8,128)(2,1)S(1)}, u32[]{:S(2)}, u32[]{:S(2)}) collective-permute-start(bf16[144,1024]{1,0:T(8,128)(2,1)S(1)} %shard_map.64), channel_id=1, source_target_pairs={{0,2},{1,3},{2,0},{3,1},{4,6},{5,7},{6,4},{7,5},{8,10},{9,11},{10,... | collective-permute-start | bytes 884744 | tf_op jit(solution)/shard_map/ppermute | solution.py:382
  50.1 6.5 %copy-start.1 = (bf16[256,512]{1,0:T(8,128)(2,1)S(1)}, bf16[256,512]{1,0:T(8,128)(2,1)}, u32[]{:S(2)}) copy-start(bf16[256,512]{1,0:T(8,128)(2,1)} %refs_1_.1) | copy-start | bytes 786436
  54.5 6.9 %collective-permute-start.10 = (bf16[144,1024]{1,0:T(8,128)(2,1)S(1)}, bf16[144,1024]{1,0:T(8,128)(2,1)S(1)}, u32[]{:S(2)}, u32[]{:S(2)}) collective-permute-start(bf16[144,1024]{1,0:T(8,128)(2,1)S(1)} %get-tuple-element.14), channel_id=1, source_target_pairs={{0,3},{1,0},{2,1},{3,2},{4,7},{5,4},{6,5},{7,6},{8,11},{9,8},{10,9... | collective-permute-start | bytes 884744 | tf_op jit(solution)/shard_map/ppermute | solution.py:382
  56.0 7.9 %collective-permute-start.11 = (bf16[144,1024]{1,0:T(8,128)(2,1)S(1)}, bf16[144,1024]{1,0:T(8,128)(2,1)S(1)}, u32[]{:S(2)}, u32[]{:S(2)}) collective-permute-start(bf16[144,1024]{1,0:T(8,128)(2,1)S(1)} %get-tuple-element.15), channel_id=1, source_target_pairs={{0,1},{1,2},{2,3},{3,0},{4,5},{5,6},{6,7},{7,4},{8,9},{9,10},{10,1... | collective-permute-start | bytes 884744 | tf_op jit(solution)/shard_map/ppermute | solution.py:382
where the time goes:
time: 64.5 us; the launch traced here: 64.9 us
  starting transfers between devices  33.1 us (51%)
  Pallas kernels  22.4 us (35%)
  waiting for transfers between devices  8.46 us (13%)
  between operations  0.85 us (1%)
    ppermute x8, starting transfers between devices, move(): return lax.ppermute(block, 'ctx', along)  23.7 us
    pallas_call x5, Pallas kernels, run_attend(): pl.pallas_call(functools.partial(attend, steps, places, carry is not None...  19.8 us
    ppermute x3, starting transfers between devices, shards(): others = [lax.ppermute(queries, 'ctx', y_pairs(-s)) for s in steps]  7.22 us
    ppermute x8, waiting for transfers between devices, move(): return lax.ppermute(block, 'ctx', along)  5.47 us
    ppermute x3, waiting for transfers between devices, shards(): lax.ppermute(m, 'ctx', y_pairs(s))  2.99 us
    ppermute x3, starting transfers between devices, shards(): lax.ppermute(m, 'ctx', y_pairs(s))  2.2 us
    pallas_call x1, Pallas kernels, run_turn(): pl.pallas_call(kernel, out_shape=jax.ShapeDtypeStruct(shape, jnp.bfloat16...  1.6 us
  transfers between devices with their start and end apart: 14, of which 3 were waited for; matrix products, arithmetic and copies ran while one was open for 0% of the time, Pallas kernels for 27%

commit v1 on v0

--- a/solution.py
+++ b/solution.py
@@ -120,7 +120,7 @@
     nb = len(flat)
     refs = list(refs)
     lengths_ref = refs.pop(0)
-    q_refs = [refs.pop(0) for _ in range(nq)]
+    q_refs = [refs.pop(0) for _ in range(1 if carried else nq)]
     kv_refs = [refs.pop(0) for _ in places]
     if carried:
         acc_in, top_in = refs.pop(0), refs.pop(0)
@@ -129,7 +129,8 @@
         acc, top = refs.pop(), refs.pop()
     else:
         acc, top = refs.pop(0), refs.pop(0)
-    qt, ks, vt, key_at, seen = refs
+    qt = q_refs[0] if carried else refs.pop(0)
+    ks, vt, key_at, seen = refs
 
     me = lax.axis_index("ctx")
     x, z, y = me // (Z * Y), (me // Y) % Z, me % Y
@@ -138,7 +139,7 @@
     row_high = row_low + (ROW_SPAN - 1)
     low = doc_start(lengths_ref, row_low)
 
-    for n in range(nq):
+    for n in range(0 if carried else nq):
         for h in range(HEADS):
             scaled = q_refs[n][:, h * DIM : (h + 1) * DIM].T.astype(jnp.float32) * EXP2_SCALE
             high = scaled.astype(jnp.bfloat16)
@@ -292,7 +293,6 @@
     acc = jax.ShapeDtypeStruct((tiles, EXT, ROWS), jnp.float32)
     top = jax.ShapeDtypeStruct((tiles, 1, ROWS), jnp.float32)
     scratch = [
-        pltpu.VMEM((tiles, 2 * DIM, ROWS), jnp.bfloat16),
         pltpu.VMEM((nb * ROWS, 2 * DIM), jnp.bfloat16),
         pltpu.VMEM((EXT, nb * ROWS), jnp.bfloat16),
         pltpu.SMEM((nb,), jnp.int32),
@@ -302,7 +302,7 @@
         out_shape = [jax.ShapeDtypeStruct((EXT, HEADS * ROWS), jnp.bfloat16)] * nq
         scratch += [pltpu.VMEM(top.shape, top.dtype), pltpu.VMEM(acc.shape, acc.dtype)]
     else:
-        out_shape = [acc, top]
+        out_shape = [acc, top, jax.ShapeDtypeStruct((tiles, 2 * DIM, ROWS), jnp.bfloat16)]
     operands = [lengths, *queries, *arrays, *(carry or ())]
     units = 5 * nq * nb * HEADS * ROWS * ROWS
     return pl.pallas_call(
@@ -311,7 +311,7 @@
         in_specs=[pl.BlockSpec(memory_space=pltpu.SMEM)] + [vmem] * (len(operands) - 1),
         out_specs=[vmem] * len(out_shape),
         scratch_shapes=scratch,
-        compiler_params=pltpu.CompilerParams(vmem_limit_bytes=28 << 20),
+        compiler_params=pltpu.CompilerParams(vmem_limit_bytes=20 << 20),
         cost_estimate=pl.CostEstimate(
             flops=units * DIM * 2, bytes_accessed=1 << 20, transcendentals=units // 2
         ),
@@ -377,10 +377,10 @@
     received = []
     for low, high in ((0, 2), (2, 3)):
         group, these = steps[low:high], others[low:high]
-        carry = run_attend(lengths, these, group, *unzip(most), None, False)
-        messages = run_attend(lengths, these, group, *unzip(rest), carry, True)
+        *carry, turned = run_attend(lengths, these, group, *unzip(most), None, False)
+        messages = run_attend(lengths, [turned], group, *unzip(rest), carry, True)
         received += [lax.ppermute(m, "ctx", y_pairs(s)) for m, s in zip(messages, group)]
-    acc, top = run_attend(lengths, [queries], (0,), *unzip(most + rest), None, False)
+    acc, top, _ = run_attend(lengths, [queries], (0,), *unzip(most + rest), None, False)
     return tuple(run_merge(acc, top, received))
 
 

time: 64.5 us -> 65.1 us (level)
  Pallas kernels: 22.4 us -> 23.2 us
    pallas_call x5, Pallas kernels: 19.8 us -> 20.6 us  [run_attend(): pl.pallas_call(functools.partial(attend, steps, places, carry is not None...]
  transfers between devices with their start and end apart: 14 -> 14, of which waited for: 3 -> 2; matrix products, arithmetic and copies ran while one was open for 0% -> 0% of each run, Pallas kernels for 27% -> 28%
where the time goes in v1:
time: 65.1 us; the launch traced here: 65.5 us
  starting transfers between devices  33.1 us (51%)
  Pallas kernels  23.2 us (36%)
  waiting for transfers between devices  8.26 us (13%)
  between operations  0.83 us (1%)
    ppermute x8, starting transfers between devices, move(): return lax.ppermute(block, 'ctx', along)  23.7 us
    pallas_call x5, Pallas kernels, run_attend(): pl.pallas_call(functools.partial(attend, steps, places, carry is not None...  20.6 us
    ppermute x3, starting transfers between devices, shards(): others = [lax.ppermute(queries, 'ctx', y_pairs(-s)) for s in steps]  7.22 us
    ppermute x8, waiting for transfers between devices, move(): return lax.ppermute(block, 'ctx', along)  5.47 us
    ppermute x3, waiting for transfers between devices, shards(): lax.ppermute(m, 'ctx', y_pairs(s))  2.78 us
    ppermute x3, starting transfers between devices, shards(): lax.ppermute(m, 'ctx', y_pairs(s))  2.2 us
    pallas_call x1, Pallas kernels, run_turn(): pl.pallas_call(kernel, out_shape=jax.ShapeDtypeStruct(shape, jnp.bfloat16...  1.6 us
  transfers between devices with their start and end apart: 14, of which 2 were waited for; matrix products, arithmetic and copies ran while one was open for 0% of the time, Pallas kernels for 28%

profile of v1, /device:TPU:6, one launch (start us, length us, event | category | flops | bytes accessed | tf_op | source)
XLA Modules:
  0.0 65.5 jit_solution(15227442617528200450)
XLA Ops:
  0.6 1.6 %shard_map.59.refs_2_.refs_3_ = bf16[512,128]{1,0:T(8,128)(2,1)} custom-call(bf16[256,128]{1,0:T(8,128)(2,1)} %k_ref.1, bf16[256,128]{1,0:T(8,128)(2,1)} %v_ref.1), custom_call_target="tpu_custom_call" | custom-call | tf_op jit(solution)/shard_map/pallas_call | solution.py:330
  2.2 3.9 %collective-permute-start = (bf16[512,128]{1,0:T(8,128)(2,1)}, bf16[512,128]{1,0:T(8,128)(2,1)S(1)}, u32[]{:S(2)}, u32[]{:S(2)}) collective-permute-start(bf16[512,128]{1,0:T(8,128)(2,1)} %shard_map.59.refs_2_.refs_3_), channel_id=1, source_target_pairs={{0,4},{1,5},{2,6},{3,7},{4,8},{5,9},{6,10},{7,11},{8,12},{9,13},{1... | collective-permute-start | bytes 393224 | tf_op jit(solution)/shard_map/ppermute | solution.py:53
  6.2 1.3 %collective-permute-start.1 = (bf16[512,128]{1,0:T(8,128)(2,1)}, bf16[512,128]{1,0:T(8,128)(2,1)S(1)}, u32[]{:S(2)}, u32[]{:S(2)}) collective-permute-start(bf16[512,128]{1,0:T(8,128)(2,1)} %shard_map.59.refs_2_.refs_3_), channel_id=1, source_target_pairs={{0,36},{1,37},{2,38},{3,39},{4,40},{5,41},{6,42},{7,43},{8,44},{9,... | collective-permute-start | bytes 393224 | tf_op jit(solution)/shard_map/ppermute | solution.py:53
  7.5 5.2 %collective-permute-start.2 = (bf16[512,128]{1,0:T(8,128)(2,1)}, bf16[512,128]{1,0:T(8,128)(2,1)S(1)}, u32[]{:S(2)}, u32[]{:S(2)}) collective-permute-start(bf16[512,128]{1,0:T(8,128)(2,1)} %shard_map.59.refs_2_.refs_3_), channel_id=1, source_target_pairs={{4,32},{5,33},{6,34},{7,35},{8,36},{9,37},{10,38},{11,39},{12,40},... | collective-permute-start | bytes 393224 | tf_op jit(solution)/shard_map/ppermute | solution.py:53
  12.7 4.3 %collective-permute-start.3 = (bf16[512,128]{1,0:T(8,128)(2,1)}, bf16[512,128]{1,0:T(8,128)(2,1)S(1)}, u32[]{:S(2)}, u32[]{:S(2)}) collective-permute-start(bf16[512,128]{1,0:T(8,128)(2,1)} %shard_map.59.refs_2_.refs_3_), channel_id=1, source_target_pairs={{0,16},{1,17},{2,18},{3,19},{4,20},{5,21},{6,22},{7,23},{8,24},{9,... | collective-permute-start | bytes 393224 | tf_op jit(solution)/shard_map/ppermute | solution.py:53
  17.0 3.3 %collective-permute-start.12 = (bf16[256,512]{1,0:T(8,128)(2,1)}, bf16[256,512]{1,0:T(8,128)(2,1)S(1)}, u32[]{:S(2)}, u32[]{:S(2)}) collective-permute-start(bf16[256,512]{1,0:T(8,128)(2,1)} %refs_1_.1), channel_id=1, source_target_pairs={{0,2},{1,3},{2,0},{3,1},{4,6},{5,7},{6,4},{7,5},{8,10},{9,11},{10,... | collective-permute-start | bytes 786440 | tf_op jit(solution)/shard_map/ppermute | solution.py:376
  20.3 0.7 %collective-permute-start.4 = (bf16[512,128]{1,0:T(8,128)(2,1)}, bf16[512,128]{1,0:T(8,128)(2,1)S(1)}, u32[]{:S(2)}, u32[]{:S(2)}) collective-permute-start(bf16[512,128]{1,0:T(8,128)(2,1)} %shard_map.59.refs_2_.refs_3_), channel_id=1, source_target_pairs={{4,28},{5,29},{6,30},{7,31},{36,60},{37,61},{38,62},{39,63},{68,92... | collective-permute-start | bytes 393224 | tf_op jit(solution)/shard_map/ppermute | solution.py:53
  21.0 1.3 %collective-permute-start.5 = (bf16[512,128]{1,0:T(8,128)(2,1)}, bf16[512,128]{1,0:T(8,128)(2,1)S(1)}, u32[]{:S(2)}, u32[]{:S(2)}) collective-permute-start(bf16[512,128]{1,0:T(8,128)(2,1)} %shard_map.59.refs_2_.refs_3_), channel_id=1, source_target_pairs={{16,28},{17,29},{18,30},{19,31},{48,60},{49,61},{50,62},{51,63},{1... | collective-permute-start | bytes 393224 | tf_op jit(solution)/shard_map/ppermute | solution.py:53
  22.3 0.8 %collective-permute-start.8 = (bf16[256,512]{1,0:T(8,128)(2,1)}, bf16[256,512]{1,0:T(8,128)(2,1)S(1)}, u32[]{:S(2)}, u32[]{:S(2)}) collective-permute-start(bf16[256,512]{1,0:T(8,128)(2,1)} %refs_1_.1), channel_id=1, source_target_pairs={{0,1},{1,2},{2,3},{3,0},{4,5},{5,6},{6,7},{7,4},{8,9},{9,10},{10,1... | collective-permute-start | bytes 786440 | tf_op jit(solution)/shard_map/ppermute | solution.py:376
  23.0 5.4 %collective-permute-done.3.refs_6_.refs_7_ = bf16[512,128]{1,0:T(8,128)(2,1)S(1)} collective-permute-done((bf16[512,128]{1,0:T(8,128)(2,1)}, bf16[512,128]{1,0:T(8,128)(2,1)S(1)}, u32[]{:S(2)}, u32[]{:S(2)}) %collective-permute-start.3) | collective-permute-done | bytes 131104 | tf_op jit(solution)/shard_map/ppermute | solution.py:53
  28.5 3.2 %collective-permute-start.9 = (bf16[256,512]{1,0:T(8,128)(2,1)}, bf16[256,512]{1,0:T(8,128)(2,1)S(1)}, u32[]{:S(2)}, u32[]{:S(2)}) collective-permute-start(bf16[256,512]{1,0:T(8,128)(2,1)} %refs_1_.1), channel_id=1, source_target_pairs={{0,3},{1,0},{2,1},{3,2},{4,7},{5,4},{6,5},{7,6},{8,11},{9,8},{10,9... | collective-permute-start | bytes 786440 | tf_op jit(solution)/shard_map/ppermute | solution.py:376
  31.7 0.1 pad_maximum_fusion.1
  31.7 3.3 %collective-permute-start.6 = (bf16[1536,128]{1,0:T(8,128)(2,1)S(1)}, bf16[1536,128]{1,0:T(8,128)(2,1)S(1)}, u32[]{:S(2)}, u32[]{:S(2)}) collective-permute-start(bf16[1536,128]{1,0:T(8,128)(2,1)S(1)} %get-tuple-element.23), channel_id=1, source_target_pairs={{4,8},{5,9},{6,10},{7,11},{8,12},{9,13},{10,14},{11,15},{12,16},{1... | collective-permute-start | bytes 1179656 | tf_op jit(solution)/shard_map/ppermute | solution.py:53
  35.0 3.8 %collective-permute-start.7 = (bf16[1536,128]{1,0:T(8,128)(2,1)S(1)}, bf16[1536,128]{1,0:T(8,128)(2,1)S(1)}, u32[]{:S(2)}, u32[]{:S(2)}) collective-permute-start(bf16[1536,128]{1,0:T(8,128)(2,1)S(1)} %get-tuple-element.22), channel_id=1, source_target_pairs={{16,12},{17,13},{18,14},{19,15},{20,16},{21,17},{22,18},{23,19},{2... | collective-permute-start | bytes 1179656 | tf_op jit(solution)/shard_map/ppermute | solution.py:53
  38.8 3.1 %shard_map.63 = (f32[4,144,256]{2,1,0:T(8,128)S(1)}, f32[4,1,256]{2,1,0:T(1,128)S(1)}, bf16[4,256,256]{2,1,0:T(8,128)(2,1)S(1)}) custom-call(s32[8]{0:T(128)S(1)} %copy-done.2, bf16[256,512]{1,0:T(8,128)(2,1)S(1)} %collective-permute-done.12.refs_1_, bf16[512,128]{1,0:T(8,128)(2,1)S(1)} %copy-done, ...), custom_call_target="tpu_custom_call" | custom-call | flops 2348810240 | bytes 1048576 | tf_op jit(solution)/shard_map/pallas_call | solution.py:308
  42.0 5.7 %shard_map.61 = (f32[8,144,256]{2,1,0:T(8,128)S(1)}, f32[8,1,256]{2,1,0:T(1,128)S(1)}, bf16[8,256,256]{2,1,0:T(8,128)(2,1)S(1)}) custom-call(s32[8]{0:T(128)S(1)} %copy-done.2, bf16[256,512]{1,0:T(8,128)(2,1)S(1)} %collective-permute-done.8.refs_1_, bf16[256,512]{1,0:T(8,128)(2,1)S(1)} %collective-permute-done.9.refs_2_, bf16[512,128]{1,0:T(8,128)(2,1)S(1)} %copy-done, ...), custom_call_target="tpu_custom_call" | custom-call | flops 4697620480 | bytes 1048576 | tf_op jit(solution)/shard_map/pallas_call | solution.py:308
  47.7 2.3 %shard_map.64 = bf16[144,1024]{1,0:T(8,128)(2,1)S(1)} custom-call(s32[8]{0:T(128)S(1)} %copy-done.2, bf16[4,256,256]{2,1,0:T(8,128)(2,1)S(1)} %get-tuple-element.19.refs_1_, bf16[1536,128]{1,0:T(8,128)(2,1)S(1)} %collective-permute-done.6.refs_9_.refs_2_, bf16[1536,128]{1,0:T(8,128)(2,1)S(1)} %collective-permute-done.7.refs_10_.refs_3_, ...), custom_call_target="tpu_custom_call" | custom-call | flops 2013265920 | bytes 1048576 | tf_op jit(solution)/shard_map/pallas_call | solution.py:308
  50.1 0.1 collective-permute-start.13
  50.2 4.2 %shard_map.62 = (bf16[144,1024]{1,0:T(8,128)(2,1)S(1)}, bf16[144,1024]{1,0:T(8,128)(2,1)S(1)}) custom-call(s32[8]{0:T(128)S(1)} %copy-done.2, bf16[8,256,256]{2,1,0:T(8,128)(2,1)S(1)} %get-tuple-element.14.refs_1_, bf16[1536,128]{1,0:T(8,128)(2,1)S(1)} %collective-permute-done.6.refs_9_.refs_2_, ...), custom_call_target="tpu_custom_call" | custom-call | flops 4026531840 | bytes 1048576 | tf_op jit(solution)/shard_map/pallas_call | solution.py:308
  54.4 0.9 %collective-permute-start.10 = (bf16[144,1024]{1,0:T(8,128)(2,1)S(1)}, bf16[144,1024]{1,0:T(8,128)(2,1)S(1)}, u32[]{:S(2)}, u32[]{:S(2)}) collective-permute-start(bf16[144,1024]{1,0:T(8,128)(2,1)S(1)} %get-tuple-element.17), channel_id=1, source_target_pairs={{0,3},{1,0},{2,1},{3,2},{4,7},{5,4},{6,5},{7,6},{8,11},{9,8},{10,9... | collective-permute-start | bytes 884744 | tf_op jit(solution)/shard_map/ppermute | solution.py:382
  55.3 1.2 %collective-permute-start.11 = (bf16[144,1024]{1,0:T(8,128)(2,1)S(1)}, bf16[144,1024]{1,0:T(8,128)(2,1)S(1)}, u32[]{:S(2)}, u32[]{:S(2)}) collective-permute-start(bf16[144,1024]{1,0:T(8,128)(2,1)S(1)} %get-tuple-element.18), channel_id=1, source_target_pairs={{0,1},{1,2},{2,3},{3,0},{4,5},{5,6},{6,7},{7,4},{8,9},{9,10},{10,1... | collective-permute-start | bytes 884744 | tf_op jit(solution)/shard_map/ppermute | solution.py:382
  56.5 5.2 %shard_map.60 = (f32[4,144,256]{2,1,0:T(8,128)S(1)}, f32[4,1,256]{2,1,0:T(1,128)S(1)}, bf16[4,256,256]{2,1,0:T(8,128)(2,1)}) custom-call(s32[8]{0:T(128)S(1)} %copy-done.2, bf16[256,512]{1,0:T(8,128)(2,1)S(1)} %copy-done.1, bf16[512,128]{1,0:T(8,128)(2,1)S(1)} %copy-done, bf16[512,128]{1,0:T(8,128)(2,1)S(1)} %collective-permute-done.refs_3_.refs_4_, ...), custom_call_target="tpu_custom_call" | custom-call | flops 4362076160 | bytes 1048576 | tf_op jit(solution)/shard_map/pallas_call | solution.py:308
  61.7 2.8 %collective-permute-done.11.refs_1_ = bf16[144,1024]{1,0:T(8,128)(2,1)S(1)} collective-permute-done((bf16[144,1024]{1,0:T(8,128)(2,1)S(1)}, bf16[144,1024]{1,0:T(8,128)(2,1)S(1)}, u32[]{:S(2)}, u32[]{:S(2)}) %collective-permute-start.11) | collective-permute-done | bytes 294944 | tf_op jit(solution)/shard_map/ppermute | solution.py:382
  64.5 1.0 %shard_map.65 = (bf16[256,512]{1,0:T(8,128)(2,1)}, f32[4,256]{1,0:T(4,128)}) custom-call(f32[4,144,256]{2,1,0:T(8,128)S(1)} %get-tuple-element.12.acc, f32[4,1,256]{2,1,0:T(1,128)S(1)} %get-tuple-element.13.top, bf16[144,1024]{1,0:T(8,128)(2,1)S(1)} %collective-permute-done.10.refs_0_, bf16[144,1024]{1,0:T(8,128)(2,1)S(1)} %collective-permute-done.11.refs_1_, ...), custom_call_target="tpu_custom_call" | custom-call | tf_op jit(solution)/shard_map/pallas_call | solution.py:359
  (18 shorter events, 0.0 us)
Async XLA Ops:
  0.6 38.2 %copy-start.2 = (s32[8]{0:T(128)S(1)}, s32[8]{0:T(128)}, u32[]{:S(2)}) copy-start(s32[8]{0:T(128)} %refs_0_.9) | copy-start | bytes 100
  2.2 36.6 %copy-start = (bf16[512,128]{1,0:T(8,128)(2,1)S(1)}, bf16[512,128]{1,0:T(8,128)(2,1)}, u32[]{:S(2)}) copy-start(bf16[512,128]{1,0:T(8,128)(2,1)} %shard_map.59.refs_2_.refs_3_) | copy-start | bytes 393220
  2.2 18.0 %collective-permute-start = (bf16[512,128]{1,0:T(8,128)(2,1)}, bf16[512,128]{1,0:T(8,128)(2,1)S(1)}, u32[]{:S(2)}, u32[]{:S(2)}) collective-permute-start(bf16[512,128]{1,0:T(8,128)(2,1)} %shard_map.59.refs_2_.refs_3_), channel_id=1, source_target_pairs={{0,4},{1,5},{2,6},{3,7},{4,8},{5,9},{6,10},{7,11},{8,12},{9,13},{1... | collective-permute-start | bytes 393224 | tf_op jit(solution)/shard_map/ppermute | solution.py:53
  6.2 14.8 %collective-permute-start.1 = (bf16[512,128]{1,0:T(8,128)(2,1)}, bf16[512,128]{1,0:T(8,128)(2,1)S(1)}, u32[]{:S(2)}, u32[]{:S(2)}) collective-permute-start(bf16[512,128]{1,0:T(8,128)(2,1)} %shard_map.59.refs_2_.refs_3_), channel_id=1, source_target_pairs={{0,36},{1,37},{2,38},{3,39},{4,40},{5,41},{6,42},{7,43},{8,44},{9,... | collective-permute-start | bytes 393224 | tf_op jit(solution)/shard_map/ppermute | solution.py:53
  7.5 14.8 %collective-permute-start.2 = (bf16[512,128]{1,0:T(8,128)(2,1)}, bf16[512,128]{1,0:T(8,128)(2,1)S(1)}, u32[]{:S(2)}, u32[]{:S(2)}) collective-permute-start(bf16[512,128]{1,0:T(8,128)(2,1)} %shard_map.59.refs_2_.refs_3_), channel_id=1, source_target_pairs={{4,32},{5,33},{6,34},{7,35},{8,36},{9,37},{10,38},{11,39},{12,40},... | collective-permute-start | bytes 393224 | tf_op jit(solution)/shard_map/ppermute | solution.py:53
  12.7 15.7 %collective-permute-start.3 = (bf16[512,128]{1,0:T(8,128)(2,1)}, bf16[512,128]{1,0:T(8,128)(2,1)S(1)}, u32[]{:S(2)}, u32[]{:S(2)}) collective-permute-start(bf16[512,128]{1,0:T(8,128)(2,1)} %shard_map.59.refs_2_.refs_3_), channel_id=1, source_target_pairs={{0,16},{1,17},{2,18},{3,19},{4,20},{5,21},{6,22},{7,23},{8,24},{9,... | collective-permute-start | bytes 393224 | tf_op jit(solution)/shard_map/ppermute | solution.py:53
  17.0 21.8 %collective-permute-start.12 = (bf16[256,512]{1,0:T(8,128)(2,1)}, bf16[256,512]{1,0:T(8,128)(2,1)S(1)}, u32[]{:S(2)}, u32[]{:S(2)}) collective-permute-start(bf16[256,512]{1,0:T(8,128)(2,1)} %refs_1_.1), channel_id=1, source_target_pairs={{0,2},{1,3},{2,0},{3,1},{4,6},{5,7},{6,4},{7,5},{8,10},{9,11},{10,... | collective-permute-start | bytes 786440 | tf_op jit(solution)/shard_map/ppermute | solution.py:376
  20.3 11.4 %collective-permute-start.4 = (bf16[512,128]{1,0:T(8,128)(2,1)}, bf16[512,128]{1,0:T(8,128)(2,1)S(1)}, u32[]{:S(2)}, u32[]{:S(2)}) collective-permute-start(bf16[512,128]{1,0:T(8,128)(2,1)} %shard_map.59.refs_2_.refs_3_), channel_id=1, source_target_pairs={{4,28},{5,29},{6,30},{7,31},{36,60},{37,61},{38,62},{39,63},{68,92... | collective-permute-start | bytes 393224 | tf_op jit(solution)/shard_map/ppermute | solution.py:53
  21.0 14.1 %collective-permute-start.5 = (bf16[512,128]{1,0:T(8,128)(2,1)}, bf16[512,128]{1,0:T(8,128)(2,1)S(1)}, u32[]{:S(2)}, u32[]{:S(2)}) collective-permute-start(bf16[512,128]{1,0:T(8,128)(2,1)} %shard_map.59.refs_2_.refs_3_), channel_id=1, source_target_pairs={{16,28},{17,29},{18,30},{19,31},{48,60},{49,61},{50,62},{51,63},{1... | collective-permute-start | bytes 393224 | tf_op jit(solution)/shard_map/ppermute | solution.py:53
  22.3 19.7 %collective-permute-start.8 = (bf16[256,512]{1,0:T(8,128)(2,1)}, bf16[256,512]{1,0:T(8,128)(2,1)S(1)}, u32[]{:S(2)}, u32[]{:S(2)}) collective-permute-start(bf16[256,512]{1,0:T(8,128)(2,1)} %refs_1_.1), channel_id=1, source_target_pairs={{0,1},{1,2},{2,3},{3,0},{4,5},{5,6},{6,7},{7,4},{8,9},{9,10},{10,1... | collective-permute-start | bytes 786440 | tf_op jit(solution)/shard_map/ppermute | solution.py:376
  28.5 13.5 %collective-permute-start.9 = (bf16[256,512]{1,0:T(8,128)(2,1)}, bf16[256,512]{1,0:T(8,128)(2,1)S(1)}, u32[]{:S(2)}, u32[]{:S(2)}) collective-permute-start(bf16[256,512]{1,0:T(8,128)(2,1)} %refs_1_.1), channel_id=1, source_target_pairs={{0,3},{1,0},{2,1},{3,2},{4,7},{5,4},{6,5},{7,6},{8,11},{9,8},{10,9... | collective-permute-start | bytes 786440 | tf_op jit(solution)/shard_map/ppermute | solution.py:376
  31.7 16.0 %collective-permute-start.6 = (bf16[1536,128]{1,0:T(8,128)(2,1)S(1)}, bf16[1536,128]{1,0:T(8,128)(2,1)S(1)}, u32[]{:S(2)}, u32[]{:S(2)}) collective-permute-start(bf16[1536,128]{1,0:T(8,128)(2,1)S(1)} %get-tuple-element.23), channel_id=1, source_target_pairs={{4,8},{5,9},{6,10},{7,11},{8,12},{9,13},{10,14},{11,15},{12,16},{1... | collective-permute-start | bytes 1179656 | tf_op jit(solution)/shard_map/ppermute | solution.py:53
  35.0 12.7 %collective-permute-start.7 = (bf16[1536,128]{1,0:T(8,128)(2,1)S(1)}, bf16[1536,128]{1,0:T(8,128)(2,1)S(1)}, u32[]{:S(2)}, u32[]{:S(2)}) collective-permute-start(bf16[1536,128]{1,0:T(8,128)(2,1)S(1)} %get-tuple-element.22), channel_id=1, source_target_pairs={{16,12},{17,13},{18,14},{19,15},{20,16},{21,17},{22,18},{23,19},{2... | collective-permute-start | bytes 1179656 | tf_op jit(solution)/shard_map/ppermute | solution.py:53
  50.1 11.7 %collective-permute-start.13 = (bf16[144,1024]{1,0:T(8,128)(2,1)S(1)}, bf16[144,1024]{1,0:T(8,128)(2,1)S(1)}, u32[]{:S(2)}, u32[]{:S(2)}) collective-permute-start(bf16[144,1024]{1,0:T(8,128)(2,1)S(1)} %shard_map.64), channel_id=1, source_target_pairs={{0,2},{1,3},{2,0},{3,1},{4,6},{5,7},{6,4},{7,5},{8,10},{9,11},{10,... | collective-permute-start | bytes 884744 | tf_op jit(solution)/shard_map/ppermute | solution.py:382
  50.2 6.3 %copy-start.1 = (bf16[256,512]{1,0:T(8,128)(2,1)S(1)}, bf16[256,512]{1,0:T(8,128)(2,1)}, u32[]{:S(2)}) copy-start(bf16[256,512]{1,0:T(8,128)(2,1)} %refs_1_.1) | copy-start | bytes 786436
  54.4 7.3 %collective-permute-start.10 = (bf16[144,1024]{1,0:T(8,128)(2,1)S(1)}, bf16[144,1024]{1,0:T(8,128)(2,1)S(1)}, u32[]{:S(2)}, u32[]{:S(2)}) collective-permute-start(bf16[144,1024]{1,0:T(8,128)(2,1)S(1)} %get-tuple-element.17), channel_id=1, source_target_pairs={{0,3},{1,0},{2,1},{3,2},{4,7},{5,4},{6,5},{7,6},{8,11},{9,8},{10,9... | collective-permute-start | bytes 884744 | tf_op jit(solution)/shard_map/ppermute | solution.py:382
  55.3 9.2 %collective-permute-start.11 = (bf16[144,1024]{1,0:T(8,128)(2,1)S(1)}, bf16[144,1024]{1,0:T(8,128)(2,1)S(1)}, u32[]{:S(2)}, u32[]{:S(2)}) collective-permute-start(bf16[144,1024]{1,0:T(8,128)(2,1)S(1)} %get-tuple-element.18), channel_id=1, source_target_pairs={{0,1},{1,2},{2,3},{3,0},{4,5},{5,6},{6,7},{7,4},{8,9},{9,10},{10,1... | collective-permute-start | bytes 884744 | tf_op jit(solution)/shard_map/ppermute | solution.py:382
